TPU v7x, 128 devices: a whole 4x4x4 slice. The times are simulated.
128 devices in a mesh: gy: 8 (over x, core), gz: 16 (over y, z).
Axes of the slice: x: 4, y: 4, z: 4, core: 2. Of those that a mesh axis runs over, the one named last changes fastest.
Arguments:
- velocity: float32 [3, 768, 12288], P(None, 'gy', 'gz'), may hold values from -250 to 250
- strain: bfloat16 [6, 768, 12288], P(None, 'gy', 'gz'), may hold values from -250 to 250
- cell_height: float32 [768], P('gy'), may hold values from 0.5 to 2
- stencil_reach: int32 [2, 768], P(None, 'gy'), may hold values from 1 to 8, as said below
Outputs:
- coefficient: float32 [768], P('gy')
Inputs may be any that keep to these rules, and one draw needn't show every extreme that they name: `stencil_reach`: in every draw some plane reaches 8 planes on both sides; stencils are cut at the walls by the steps.
All inputs are finite; a program needn't handle non-finite values.
Results may differ from a plain program's by a relative error of at most 0.0003.
Values sent between devices are 32-bit elements; how exact they have to be, the bound alone decides.
No kernel may reach another device: no remote copies, remote signals or barrier semaphores. Data moves between devices by JAX's collectives and lax.ppermute only.
A program may use at most 128 MiB of HBM per device.

v0:
```python
import jax
import jax.numpy as jnp
from jax import lax
from jax.sharding import PartitionSpec as P

NX = 8
HMAX = 8
LEAD_INDEX = (0, 1, 2, 0, 0, 1)
TAIL_INDEX = (0, 1, 2, 1, 2, 2)
TENSOR_WEIGHTS = (1.0, 1.0, 1.0, 2.0, 2.0, 2.0)


def extended(cells, sides, width, closed):
    for axis, dim in sides:
        count = lax.axis_size(axis)
        ends = count if closed else count - 1
        head = lax.slice_in_dim(cells, 0, width, axis=dim)
        tail = lax.slice_in_dim(cells, cells.shape[dim] - width, cells.shape[dim], axis=dim)
        cells = jnp.concatenate(
            [
                lax.ppermute(tail, axis, [(i, (i + 1) % count) for i in range(ends)]),
                cells,
                lax.ppermute(head, axis, [((i + 1) % count, i) for i in range(ends)]),
            ],
            axis=dim,
        )
    return cells


def strain_rate(tensor):
    squares = 2.0 * (tensor[0] * tensor[0] + tensor[1] * tensor[1] + tensor[2] * tensor[2])
    squares = squares + 4.0 * (
        tensor[3] * tensor[3] + tensor[4] * tensor[4] + tensor[5] * tensor[5]
    )
    return jnp.sqrt(squares)


def form_fields(velocity, tensor):
    products = jnp.stack(
        [
            velocity[first_index] * velocity[second_index]
            for first_index, second_index in zip(LEAD_INDEX, TAIL_INDEX)
        ]
    )
    magnitude = strain_rate(tensor)
    return jnp.concatenate([velocity, products, tensor, magnitude[None] * tensor], axis=0)


def streamwise_filter(fields):
    length = fields.shape[-1]
    position = jnp.arange(length, dtype=jnp.int32) % NX
    behind = jnp.where(
        position == 0, jnp.roll(fields, 1 - NX, axis=-1), jnp.roll(fields, 1, axis=-1)
    )
    ahead_cells = jnp.where(
        position == NX - 1, jnp.roll(fields, NX - 1, axis=-1), jnp.roll(fields, -1, axis=-1)
    )
    return 0.25 * behind + 0.5 * fields + 0.25 * ahead_cells


def spanwise_filter(widened):
    return (
        0.25 * widened[..., : -2 * NX] + 0.5 * widened[..., NX:-NX] + 0.25 * widened[..., 2 * NX :]
    )


def band_apply(band_matrix, padded):
    flattened = padded.reshape(padded.shape[0], padded.shape[1], -1)
    result = jnp.einsum("jc,fcm->fjm", band_matrix, flattened, precision=lax.Precision.HIGHEST)
    return result.reshape((padded.shape[0], band_matrix.shape[0]) + padded.shape[2:])


def contraction(filtered, sum_axes):
    velocity_bar = filtered[0:3]
    product_bar = filtered[3:9]
    tensor_bar = filtered[9:15]
    model_bar = filtered[15:21]
    rate_bar = strain_rate(tensor_bar)
    numerator = jnp.zeros(filtered.shape[1:], jnp.float32)
    denominator = jnp.zeros(filtered.shape[1:], jnp.float32)
    for component in range(6):
        leonard = (
            product_bar[component]
            - velocity_bar[LEAD_INDEX[component]] * velocity_bar[TAIL_INDEX[component]]
        )
        model_term = model_bar[component] - 4.0 * rate_bar * tensor_bar[component]
        numerator = numerator + TENSOR_WEIGHTS[component] * leonard * model_term
        denominator = denominator + TENSOR_WEIGHTS[component] * model_term * model_term
    return (jnp.sum(numerator, axis=sum_axes), jnp.sum(denominator, axis=sum_axes))


def local(velocity, strain, cell_height, stencil_reach):
    planes = velocity.shape[1]
    cell_count = velocity.shape[2]
    total_planes = lax.axis_size("gy") * planes
    total_cells = lax.axis_size("gz") * cell_count
    heights = extended(cell_height, (("gy", 0),), HMAX, False)
    offset = lax.axis_index("gy") * planes
    rows_global = offset + jnp.arange(planes, dtype=jnp.int32)
    columns_global = offset - HMAX + jnp.arange(planes + 2 * HMAX, dtype=jnp.int32)
    lowest = jnp.maximum(rows_global - stencil_reach[0], 0)
    highest = jnp.minimum(rows_global + stencil_reach[1], total_planes - 1)
    inside = (columns_global[None, :] >= lowest[:, None]) & (
        columns_global[None, :] <= highest[:, None]
    )
    weights = jnp.where(inside, heights[None, :], 0.0)
    band_matrix = weights / jnp.sum(weights, axis=1, keepdims=True)
    raw_inputs = jnp.concatenate([velocity, strain.astype(jnp.float32)], axis=0)
    fields = form_fields(raw_inputs[0:3], raw_inputs[3:9])
    widened = extended(streamwise_filter(fields), (("gz", 2),), NX, True)
    spanwise = spanwise_filter(widened)
    full_band = lax.all_gather(band_matrix, "gy", axis=0, tiled=True)
    block_count = lax.axis_size("gy")
    grouped = spanwise.reshape(spanwise.shape[0], planes, block_count, cell_count // block_count)
    padded = jnp.pad(
        lax.all_to_all(grouped, "gy", split_axis=2, concat_axis=1, tiled=True),
        ((0, 0), (HMAX, HMAX), (0, 0), (0, 0)),
    )
    sections = [
        band_apply(
            full_band[block_index * planes : (block_index + 1) * planes],
            padded[:, block_index * planes : block_index * planes + planes + 2 * HMAX],
        )
        for block_index in range(block_count)
    ]
    filtered = jnp.concatenate(sections, axis=1)
    numerator, denominator = contraction(filtered, 1)
    numerator = jnp.sum(numerator, axis=1)
    denominator = jnp.sum(denominator, axis=1)
    numerator, denominator = lax.psum((numerator, denominator), ("gy", "gz"))
    whole = numerator / total_cells / (denominator / total_cells + 1e-06)
    return lax.dynamic_slice_in_dim(whole, offset, planes)


def solution(mesh):
    in_specs = (P(None, "gy", "gz"), P(None, "gy", "gz"), P("gy"), P(None, "gy"))
    out_specs = P("gy")
    return jax.shard_map(local, mesh=mesh, in_specs=in_specs, out_specs=out_specs, check_vma=False)
```

profile of v0, /device:TPU:1, one launch (start us, length us, event | category | flops | bytes accessed | tf_op | source)
XLA Modules:
  0.0 296.6 jit_solution(2417976112965533351)
XLA Ops:
  12.0 9.7 %fusion.62 = (f32[21,96,767]{1,2,0:T(8,128)S(1)}, f32[21,96,767]{1,2,0:T(8,128)}) fusion(f32[21,96,768]{1,2,0:T(8,128)} %multiply_dynamic-update-slice_fusion), kind=kLoop, calls=%fused_computation.136 | loop fusion | bytes 24740352 | tf_op jit(solution)/shard_map/jit(_roll_static)/slice | solution.py:56
  21.7 10.9 %fusion.65 = (f32[21,96,761]{1,2,0:T(8,128)}, f32[21,96,761]{1,2,0:T(8,128)}) fusion(f32[21,96,768]{1,2,0:T(8,128)} %multiply_dynamic-update-slice_fusion), kind=kLoop, calls=%fused_computation.139 | loop fusion | bytes 24546816 | tf_op jit(solution)/shard_map/jit(_roll_static)/slice | solution.py:56
  34.5 15.5 %fusion.6 = f32[21,96,768]{1,2,0:T(8,128)S(1)} fusion(f32[21,96,7]{1,2,0:T(8,128)S(1)} %get-tuple-element.16, f32[21,96,761]{1,2,0:T(8,128)} %get-tuple-element.18, f32[21,96,767]{1,2,0:T(8,128)} %get-tuple-element.12, f32[21,96,1]{1,2,0:T(1,128)S(1)} %get-tuple-element.14, f32[21,96,761]{1,2,0:T(8,128)} %get-tuple-element.17, ...), kind=kLoop, calls=%fused_computation.9 | loop fusion | flops 17031168 | bytes 37160448 | tf_op jit(solution)/shard_map/add | solution.py:58
  50.0 2.5 collective-permute-start
  52.5 4.7 %collective-permute-start.1 = (f32[21,96,8]{1,2,0:T(8,128)S(1)}, f32[21,96,8]{1,2,0:T(8,128)S(1)}, u32[]{:S(2)}, u32[]{:S(2)}) collective-permute-start(f32[21,96,8]{1,2,0:T(8,128)S(1)} %get-tuple-element.10), channel_id=1, source_target_pairs={{1,0},{2,1},{3,2},{4,3},{5,4},{6,5},{7,6},{8,7},{9,8},{10,9},{11,1... | collective-permute-start | bytes 193544 | tf_op jit(solution)/shard_map/ppermute | solution.py:23
  57.2 2.2 collective-permute-done
  59.4 2.4 fusion.1
  61.8 3.9 %copy.31 = f32[21,96,8,96]{1,3,0,2:T(8,128)} copy(f32[21,96,8,96]{1,3,2,0:T(8,128)S(1)} %bitcast.280) | data formatting | bytes 12386304 | tf_op jit(solution)/shard_map/reshape | solution.py:114
  65.7 6.2 %all-to-all-start = ((f32[21,96,8,96]{1,3,0,2:T(8,128)}), f32[21,96,8,96]{1,3,0,2:T(8,128)}, u32[]{:S(2)}, u32[]{:S(2)}) async-start(f32[21,96,8,96]{1,3,0,2:T(8,128)} %copy.31), calls=%async_computation | async-start | bytes 16515072 | tf_op jit(solution)/shard_map/all_to_all | solution.py:116
  72.0 3.5 %collective-permute-start.2 = (f32[8]{0:T(128)S(1)}, f32[8]{0:T(128)S(1)}, u32[]{:S(2)}, u32[]{:S(2)}) collective-permute-start(f32[8]{0:T(128)S(1)} %get-tuple-element.21), channel_id=1, source_target_pairs={{0,16},{16,32},{32,48},{48,64},{64,80},{80,96},{96,112},{1,17},{17... | collective-permute-start | bytes 104 | tf_op jit(solution)/shard_map/ppermute | solution.py:21
  77.5 83.5 %collective-permute-done.2 = f32[8]{0:T(128)S(1)} collective-permute-done((f32[8]{0:T(128)S(1)}, f32[8]{0:T(128)S(1)}, u32[]{:S(2)}, u32[]{:S(2)}) %collective-permute-start.2) | collective-permute-done | bytes 64 | tf_op jit(solution)/shard_map/ppermute | solution.py:21
  160.9 2.4 collective-permute-done.3
  163.7 11.9 %all_gather.3 = f32[768,112]{1,0:T(8,128)S(1)} all-gather(f32[96,112]{1,0:T(8,128)S(1)} %select_divide_fusion), channel_id=1, replica_groups=mesh['gy'=8,'gz'=16] {'gy'}, dimensions={0}, use_global_device_ids=true | all-gather | bytes 387072 | tf_op jit(solution)/shard_map/all_gather | solution.py:112
  175.6 13.4 %copy.32 = f32[21,8,96,1,96]{2,1,4,0,3:T(8,128)} copy(f32[21,8,96,1,96]{2,4,0,1,3:T(8,128)} %bitcast.3) | data formatting | bytes 12386304 | tf_op jit(solution)/shard_map/all_to_all | solution.py:116
  189.0 9.5 %all_to_all.16 = f32[21,768,1,96]{1,3,0,2:T(8,128)} reshape(f32[21,8,96,1,96]{2,1,4,0,3:T(8,128)} %copy.32) | data formatting | bytes 12386304 | tf_op jit(solution)/shard_map/all_to_all | solution.py:116
  198.5 2.4 convolution_bitcast_fusion
  200.9 2.6 convolution_bitcast_fusion.1
  207.5 2.1 convolution_bitcast_fusion.4
  209.5 2.0 convolution_bitcast_fusion.5
  211.5 2.0 convolution_bitcast_fusion.6
  214.6 8.9 %concatenate.40 = f32[21,768,1,96]{1,3,0,2:T(8,128)} concatenate(f32[21,96,1,96]{1,3,0,2:T(8,128)S(1)} %convolution_bitcast_fusion.7, f32[21,96,1,96]{1,3,0,2:T(8,128)} %convolution_bitcast_fusion.6, f32[21,96,1,96]{1,3,0,2:T(8,128)} %convolution_bitcast_fusion.5, f32[21,96,1,96]{1,3,0,2:T(8,128)} %convolution_bitcast_fusion.4, f32[21,96,1,96]{1,3,0,2:T(8,128)} %convolution_bitcast_fusion.3, ...), dimensions={1} | concatenate | bytes 12386304 | tf_op jit(solution)/shard_map/concatenate | solution.py:126
  223.4 3.3 %fusion.30 = (f32[768]{0:T(1024)S(1)}, f32[768,96]{0,1:T(8,128)S(1)}) fusion(f32[21,768,1,96]{1,3,2,0:T(8,128)} %bitcast.278, f32[21,768,1,96]{1,3,0,2:T(8,128)} %concatenate.40), kind=kLoop, calls=%fused_computation.67 | loop fusion | flops 3906816 | bytes 6491136 | tf_op jit(solution)/shard_map/reduce_sum | solution.py:128
  226.7 2.2 fusion.24
  229.0 67.1 %all-reduce.1 = (f32[768]{0:T(1024)S(1)}, f32[768]{0:T(1024)S(1)}) all-reduce(f32[768]{0:T(1024)S(1)} %fusion.24, f32[768]{0:T(1024)S(1)} %get-tuple-element.7), channel_id=1, replica_groups=mesh['gy'=8,'gz'=16] {'gy','gz'}, use_global_device_ids=true, to_apply=%region_4.5 | all-reduce | flops 1536 | bytes 12288 | tf_op jit(solution)/shard_map/psum | solution.py:130
  (39 shorter events, 21.8 us)
Async XLA Ops:
  0.0 7.5 %copy-start.1 = (bf16[6,96,768]{2,1,0:T(8,128)(2,1)S(1)}, bf16[6,96,768]{2,1,0:T(8,128)(2,1)}, u32[]{:S(2)}) copy-start(bf16[6,96,768]{2,1,0:T(8,128)(2,1)} %param.5) | copy-start | bytes 2654212
  50.0 9.4 %collective-permute-start = (f32[21,96,8]{1,2,0:T(8,128)S(1)}, f32[21,96,8]{1,2,0:T(8,128)S(1)}, u32[]{:S(2)}, u32[]{:S(2)}) collective-permute-start(f32[21,96,8]{1,2,0:T(8,128)S(1)} %get-tuple-element.9), channel_id=1, source_target_pairs={{0,1},{1,2},{2,3},{3,4},{4,5},{5,6},{6,7},{7,8},{8,9},{9,10},{10,1... | collective-permute-start | bytes 193544 | tf_op jit(solution)/shard_map/ppermute | solution.py:21
  52.5 6.8 %collective-permute-start.1 = (f32[21,96,8]{1,2,0:T(8,128)S(1)}, f32[21,96,8]{1,2,0:T(8,128)S(1)}, u32[]{:S(2)}, u32[]{:S(2)}) collective-permute-start(f32[21,96,8]{1,2,0:T(8,128)S(1)} %get-tuple-element.10), channel_id=1, source_target_pairs={{1,0},{2,1},{3,2},{4,3},{5,4},{6,5},{7,6},{8,7},{9,8},{10,9},{11,1... | collective-permute-start | bytes 193544 | tf_op jit(solution)/shard_map/ppermute | solution.py:23
  65.7 6.2 %copy-start.2 = (f32[96]{0:T(128)S(1)}, f32[96]{0:T(128)}, u32[]{:S(2)}) copy-start(f32[96]{0:T(128)} %param.6) | copy-start | bytes 1156
  65.7 11.7 %copy-start.3 = (s32[2,96]{1,0:T(2,128)S(1)}, s32[2,96]{1,0:T(2,128)}, u32[]{:S(2)}) copy-start(s32[2,96]{1,0:T(2,128)} %param.7) | copy-start | bytes 2308
  65.7 109.9 %all-to-all-start = ((f32[21,96,8,96]{1,3,0,2:T(8,128)}), f32[21,96,8,96]{1,3,0,2:T(8,128)}, u32[]{:S(2)}, u32[]{:S(2)}) async-start(f32[21,96,8,96]{1,3,0,2:T(8,128)} %copy.31), calls=%async_computation | async-start | bytes 16515072 | tf_op jit(solution)/shard_map/all_to_all | solution.py:116
  72.0 89.0 %collective-permute-start.2 = (f32[8]{0:T(128)S(1)}, f32[8]{0:T(128)S(1)}, u32[]{:S(2)}, u32[]{:S(2)}) collective-permute-start(f32[8]{0:T(128)S(1)} %get-tuple-element.21), channel_id=1, source_target_pairs={{0,16},{16,32},{32,48},{48,64},{64,80},{80,96},{96,112},{1,17},{17... | collective-permute-start | bytes 104 | tf_op jit(solution)/shard_map/ppermute | solution.py:21
  75.5 87.8 %collective-permute-start.3 = (f32[8]{0:T(128)S(1)}, f32[8]{0:T(128)S(1)}, u32[]{:S(2)}, u32[]{:S(2)}) collective-permute-start(f32[8]{0:T(128)S(1)} %get-tuple-element.22), channel_id=1, source_target_pairs={{16,0},{32,16},{48,32},{64,48},{80,64},{96,80},{112,96},{17,1},{33... | collective-permute-start | bytes 104 | tf_op jit(solution)/shard_map/ppermute | solution.py:23
  198.5 5.0 %copy-start = (f32[21,768,1,96]{1,3,0,2:T(8,128)S(1)}, f32[21,768,1,96]{1,3,0,2:T(8,128)}, u32[]{:S(2)}) copy-start(f32[21,768,1,96]{1,3,0,2:T(8,128)} %all_to_all.16) | copy-start | bytes 18579460
where the time goes:
time: 297 us
  waiting for transfers between devices  88 us (30%)
  blocking collectives  79 us (27%)
  local copies, waits for them, and re-layouts  62.3 us (21%)
  other arithmetic  32.3 us (11%)
  starting transfers between devices  18.8 us (6%)
  matrix products  16 us (5%)
    ppermute x2, waiting for transfers between devices, extended(): lax.ppermute(tail, axis, [(i, (i + 1) % count) for i in range(ends)])  85.6 us
    psum x1, blocking collectives, local(): numerator, denominator = lax.psum((numerator, denominator), ('gy', 'gz'))  67.1 us
    all_to_all x2, local copies, waits for them, and re-layouts, local(): lax.all_to_all(grouped, 'gy', split_axis=2, concat_axis=1, tiled=True)  22.9 us
    dot_general x8, matrix products, band_apply(): jnp.einsum('jc,fcm->fjm', band_matrix, flattened, precision=lax.Precision...  16 us
    add x1, other arithmetic, streamwise_filter(): return 0.25 * behind + 0.5 * fields + 0.25 * ahead_cells  15.5 us
    all_gather x1, blocking collectives, local(): full_band = lax.all_gather(band_matrix, 'gy', axis=0, tiled=True)  11.9 us
    slice x2, local copies, waits for them, and re-layouts, streamwise_filter(): jnp.roll(fields, NX - 1, axis=-1)  11.9 us
    slice x2, local copies, waits for them, and re-layouts, streamwise_filter(): jnp.roll(fields, -1, axis=-1)  10.6 us
  transfers between devices with their start and end apart: 5, of which 3 were waited for; matrix products, arithmetic and copies ran while one was open for 0% of the time, Pallas kernels for 0%

commit v1 on v0

--- a/solution.py
+++ b/solution.py
@@ -127,7 +127,7 @@
     numerator, denominator = contraction(filtered, 1)
     numerator = jnp.sum(numerator, axis=1)
     denominator = jnp.sum(denominator, axis=1)
-    numerator, denominator = lax.psum((numerator, denominator), ("gy", "gz"))
+    numerator, denominator = lax.psum(lax.psum((numerator, denominator), "gz"), "gy")
     whole = numerator / total_cells / (denominator / total_cells + 1e-06)
     return lax.dynamic_slice_in_dim(whole, offset, planes)
 

time: 297 us -> 284 us (0.956)
  blocking collectives: 79 us -> 65.5 us
    psum x1 -> x2, blocking collectives: 67.1 us -> 53.6 us  [the longest x1 34.1 us: local(): lax.psum((numerator, denominator), 'gz')]
where the time goes in v1:
time: 284 us; the launch traced here: 283 us
  waiting for transfers between devices  88 us (31%)
  blocking collectives  65.5 us (23%)
  local copies, waits for them, and re-layouts  62.3 us (22%)
  other arithmetic  32.3 us (11%)
  starting transfers between devices  18.8 us (7%)
  matrix products  16 us (6%)
    ppermute x2, waiting for transfers between devices, extended(): lax.ppermute(tail, axis, [(i, (i + 1) % count) for i in range(ends)])  85.6 us
    psum x1, blocking collectives, local(): lax.psum((numerator, denominator), 'gz')  34.1 us
    all_to_all x2, local copies, waits for them, and re-layouts, local(): lax.all_to_all(grouped, 'gy', split_axis=2, concat_axis=1, tiled=True)  22.9 us
    psum x1, blocking collectives, local(): lax.psum(lax.psum((numerator, denominator), 'gz'), 'gy')  19.5 us
    dot_general x8, matrix products, band_apply(): jnp.einsum('jc,fcm->fjm', band_matrix, flattened, precision=lax.Precision...  16 us
    add x1, other arithmetic, streamwise_filter(): return 0.25 * behind + 0.5 * fields + 0.25 * ahead_cells  15.5 us
    all_gather x1, blocking collectives, local(): full_band = lax.all_gather(band_matrix, 'gy', axis=0, tiled=True)  11.9 us
    slice x2, local copies, waits for them, and re-layouts, streamwise_filter(): jnp.roll(fields, NX - 1, axis=-1)  11.8 us
  transfers between devices with their start and end apart: 5, of which 3 were waited for; matrix products, arithmetic and copies ran while one was open for 0% of the time, Pallas kernels for 0%

profile of v1, /device:TPU:1, one launch (start us, length us, event | category | flops | bytes accessed | tf_op | source)
XLA Modules:
  0.0 283.1 jit_solution(17385058136695054027)
XLA Ops:
  12.0 9.7 %fusion.62 = (f32[21,96,767]{1,2,0:T(8,128)S(1)}, f32[21,96,767]{1,2,0:T(8,128)}) fusion(f32[21,96,768]{1,2,0:T(8,128)} %multiply_dynamic-update-slice_fusion), kind=kLoop, calls=%fused_computation.136 | loop fusion | bytes 24740352 | tf_op jit(solution)/shard_map/jit(_roll_static)/slice | solution.py:56
  21.6 10.9 %fusion.65 = (f32[21,96,761]{1,2,0:T(8,128)}, f32[21,96,761]{1,2,0:T(8,128)}) fusion(f32[21,96,768]{1,2,0:T(8,128)} %multiply_dynamic-update-slice_fusion), kind=kLoop, calls=%fused_computation.139 | loop fusion | bytes 24546816 | tf_op jit(solution)/shard_map/jit(_roll_static)/slice | solution.py:56
  34.4 15.5 %fusion.6 = f32[21,96,768]{1,2,0:T(8,128)S(1)} fusion(f32[21,96,7]{1,2,0:T(8,128)S(1)} %get-tuple-element.18, f32[21,96,761]{1,2,0:T(8,128)} %get-tuple-element.20, f32[21,96,767]{1,2,0:T(8,128)} %get-tuple-element.14, f32[21,96,1]{1,2,0:T(1,128)S(1)} %get-tuple-element.16, f32[21,96,761]{1,2,0:T(8,128)} %get-tuple-element.19, ...), kind=kLoop, calls=%fused_computation.9 | loop fusion | flops 17031168 | bytes 37160448 | tf_op jit(solution)/shard_map/add | solution.py:58
  49.9 2.5 collective-permute-start
  52.4 4.7 %collective-permute-start.1 = (f32[21,96,8]{1,2,0:T(8,128)S(1)}, f32[21,96,8]{1,2,0:T(8,128)S(1)}, u32[]{:S(2)}, u32[]{:S(2)}) collective-permute-start(f32[21,96,8]{1,2,0:T(8,128)S(1)} %get-tuple-element.12), channel_id=1, source_target_pairs={{1,0},{2,1},{3,2},{4,3},{5,4},{6,5},{7,6},{8,7},{9,8},{10,9},{11,1... | collective-permute-start | bytes 193544 | tf_op jit(solution)/shard_map/ppermute | solution.py:23
  57.1 2.2 collective-permute-done
  59.3 2.4 fusion.1
  61.7 3.9 %copy.31 = f32[21,96,8,96]{1,3,0,2:T(8,128)} copy(f32[21,96,8,96]{1,3,2,0:T(8,128)S(1)} %bitcast.280) | data formatting | bytes 12386304 | tf_op jit(solution)/shard_map/reshape | solution.py:114
  65.7 6.2 %all-to-all-start = ((f32[21,96,8,96]{1,3,0,2:T(8,128)}), f32[21,96,8,96]{1,3,0,2:T(8,128)}, u32[]{:S(2)}, u32[]{:S(2)}) async-start(f32[21,96,8,96]{1,3,0,2:T(8,128)} %copy.31), calls=%async_computation | async-start | bytes 16515072 | tf_op jit(solution)/shard_map/all_to_all | solution.py:116
  71.9 3.5 %collective-permute-start.2 = (f32[8]{0:T(128)S(1)}, f32[8]{0:T(128)S(1)}, u32[]{:S(2)}, u32[]{:S(2)}) collective-permute-start(f32[8]{0:T(128)S(1)} %get-tuple-element.23), channel_id=1, source_target_pairs={{0,16},{16,32},{32,48},{48,64},{64,80},{80,96},{96,112},{1,17},{17... | collective-permute-start | bytes 104 | tf_op jit(solution)/shard_map/ppermute | solution.py:21
  77.4 83.5 %collective-permute-done.2 = f32[8]{0:T(128)S(1)} collective-permute-done((f32[8]{0:T(128)S(1)}, f32[8]{0:T(128)S(1)}, u32[]{:S(2)}, u32[]{:S(2)}) %collective-permute-start.2) | collective-permute-done | bytes 64 | tf_op jit(solution)/shard_map/ppermute | solution.py:21
  160.9 2.4 collective-permute-done.3
  163.6 11.9 %all_gather.3 = f32[768,112]{1,0:T(8,128)S(1)} all-gather(f32[96,112]{1,0:T(8,128)S(1)} %select_divide_fusion), channel_id=1, replica_groups=mesh['gy'=8,'gz'=16] {'gy'}, dimensions={0}, use_global_device_ids=true | all-gather | bytes 387072 | tf_op jit(solution)/shard_map/all_gather | solution.py:112
  175.5 13.4 %copy.32 = f32[21,8,96,1,96]{2,1,4,0,3:T(8,128)} copy(f32[21,8,96,1,96]{2,4,0,1,3:T(8,128)} %bitcast.3) | data formatting | bytes 12386304 | tf_op jit(solution)/shard_map/all_to_all | solution.py:116
  189.0 9.5 %all_to_all.16 = f32[21,768,1,96]{1,3,0,2:T(8,128)} reshape(f32[21,8,96,1,96]{2,1,4,0,3:T(8,128)} %copy.32) | data formatting | bytes 12386304 | tf_op jit(solution)/shard_map/all_to_all | solution.py:116
  198.4 2.4 convolution_bitcast_fusion
  200.8 2.6 convolution_bitcast_fusion.1
  207.4 2.1 convolution_bitcast_fusion.4
  211.4 2.0 convolution_bitcast_fusion.6
  214.5 8.9 %concatenate.40 = f32[21,768,1,96]{1,3,0,2:T(8,128)} concatenate(f32[21,96,1,96]{1,3,0,2:T(8,128)S(1)} %convolution_bitcast_fusion.7, f32[21,96,1,96]{1,3,0,2:T(8,128)} %convolution_bitcast_fusion.6, f32[21,96,1,96]{1,3,0,2:T(8,128)} %convolution_bitcast_fusion.5, f32[21,96,1,96]{1,3,0,2:T(8,128)} %convolution_bitcast_fusion.4, f32[21,96,1,96]{1,3,0,2:T(8,128)} %convolution_bitcast_fusion.3, ...), dimensions={1} | concatenate | bytes 12386304 | tf_op jit(solution)/shard_map/concatenate | solution.py:126
  223.3 3.3 %fusion.30 = (f32[768]{0:T(1024)S(1)}, f32[768,96]{0,1:T(8,128)S(1)}) fusion(f32[21,768,1,96]{1,3,2,0:T(8,128)} %bitcast.278, f32[21,768,1,96]{1,3,0,2:T(8,128)} %concatenate.40), kind=kLoop, calls=%fused_computation.67 | loop fusion | flops 3906816 | bytes 6491136 | tf_op jit(solution)/shard_map/reduce_sum | solution.py:128
  226.7 2.2 fusion.24
  228.9 34.1 %all-reduce.1 = (f32[768]{0:T(1024)S(1)}, f32[768]{0:T(1024)S(1)}) all-reduce(f32[768]{0:T(1024)S(1)} %fusion.24, f32[768]{0:T(1024)S(1)} %get-tuple-element.9), channel_id=1, replica_groups=mesh['gy'=8,'gz'=16] {'gz'}, use_global_device_ids=true, to_apply=%region_5.6 | all-reduce | flops 1536 | bytes 12288 | tf_op jit(solution)/shard_map/psum | solution.py:130
  263.0 19.5 %all-reduce.2 = (f32[768]{0:T(1024)S(1)}, f32[768]{0:T(1024)S(1)}) all-reduce(f32[768]{0:T(1024)S(1)} %get-tuple-element.5, f32[768]{0:T(1024)S(1)} %get-tuple-element.6), channel_id=1, replica_groups=mesh['gy'=8,'gz'=16] {'gy'}, use_global_device_ids=true, to_apply=%region_6.7 | all-reduce | flops 1536 | bytes 12288 | tf_op jit(solution)/shard_map/psum | solution.py:130
  (40 shorter events, 23.8 us)
Async XLA Ops:
  0.0 7.6 %copy-start.1 = (bf16[6,96,768]{2,1,0:T(8,128)(2,1)S(1)}, bf16[6,96,768]{2,1,0:T(8,128)(2,1)}, u32[]{:S(2)}) copy-start(bf16[6,96,768]{2,1,0:T(8,128)(2,1)} %param.5) | copy-start | bytes 2654212
  49.9 9.4 %collective-permute-start = (f32[21,96,8]{1,2,0:T(8,128)S(1)}, f32[21,96,8]{1,2,0:T(8,128)S(1)}, u32[]{:S(2)}, u32[]{:S(2)}) collective-permute-start(f32[21,96,8]{1,2,0:T(8,128)S(1)} %get-tuple-element.11), channel_id=1, source_target_pairs={{0,1},{1,2},{2,3},{3,4},{4,5},{5,6},{6,7},{7,8},{8,9},{9,10},{10,1... | collective-permute-start | bytes 193544 | tf_op jit(solution)/shard_map/ppermute | solution.py:21
  52.4 6.8 %collective-permute-start.1 = (f32[21,96,8]{1,2,0:T(8,128)S(1)}, f32[21,96,8]{1,2,0:T(8,128)S(1)}, u32[]{:S(2)}, u32[]{:S(2)}) collective-permute-start(f32[21,96,8]{1,2,0:T(8,128)S(1)} %get-tuple-element.12), channel_id=1, source_target_pairs={{1,0},{2,1},{3,2},{4,3},{5,4},{6,5},{7,6},{8,7},{9,8},{10,9},{11,1... | collective-permute-start | bytes 193544 | tf_op jit(solution)/shard_map/ppermute | solution.py:23
  65.7 6.2 %copy-start.2 = (f32[96]{0:T(128)S(1)}, f32[96]{0:T(128)}, u32[]{:S(2)}) copy-start(f32[96]{0:T(128)} %param.6) | copy-start | bytes 1156
  65.7 11.7 %copy-start.3 = (s32[2,96]{1,0:T(2,128)S(1)}, s32[2,96]{1,0:T(2,128)}, u32[]{:S(2)}) copy-start(s32[2,96]{1,0:T(2,128)} %param.7) | copy-start | bytes 2308
  65.7 109.9 %all-to-all-start = ((f32[21,96,8,96]{1,3,0,2:T(8,128)}), f32[21,96,8,96]{1,3,0,2:T(8,128)}, u32[]{:S(2)}, u32[]{:S(2)}) async-start(f32[21,96,8,96]{1,3,0,2:T(8,128)} %copy.31), calls=%async_computation | async-start | bytes 16515072 | tf_op jit(solution)/shard_map/all_to_all | solution.py:116
  71.9 89.0 %collective-permute-start.2 = (f32[8]{0:T(128)S(1)}, f32[8]{0:T(128)S(1)}, u32[]{:S(2)}, u32[]{:S(2)}) collective-permute-start(f32[8]{0:T(128)S(1)} %get-tuple-element.23), channel_id=1, source_target_pairs={{0,16},{16,32},{32,48},{48,64},{64,80},{80,96},{96,112},{1,17},{17... | collective-permute-start | bytes 104 | tf_op jit(solution)/shard_map/ppermute | solution.py:21
  75.4 87.8 %collective-permute-start.3 = (f32[8]{0:T(128)S(1)}, f32[8]{0:T(128)S(1)}, u32[]{:S(2)}, u32[]{:S(2)}) collective-permute-start(f32[8]{0:T(128)S(1)} %get-tuple-element.24), channel_id=1, source_target_pairs={{16,0},{32,16},{48,32},{64,48},{80,64},{96,80},{112,96},{17,1},{33... | collective-permute-start | bytes 104 | tf_op jit(solution)/shard_map/ppermute | solution.py:23
  198.4 5.0 %copy-start = (f32[21,768,1,96]{1,3,0,2:T(8,128)S(1)}, f32[21,768,1,96]{1,3,0,2:T(8,128)}, u32[]{:S(2)}) copy-start(f32[21,768,1,96]{1,3,0,2:T(8,128)} %all_to_all.16) | copy-start | bytes 18579460
